TPU v7x, 512 devices: a whole 4x4x16 slice. The times are simulated.
512 devices in a mesh: section: 32 (over x_hi, z), tensor: 4 (over y), dp: 4 (over x_lo, core).
Axes of the slice: x: 4 (x_hi: 2, x_lo: 2; x = x_hi * 2 + x_lo), y: 4, z: 16, core: 2. Of those that a mesh axis runs over, the one named last changes fastest.
Arguments:
- sent_acts: bfloat16 [32, 256, 3072], P('section', ('tensor', 'dp')), may hold values from -36 to 36
- sent_grads: bfloat16 [32, 256, 3072], P('section', ('tensor', 'dp')), may hold values from -0.375 to 0.375
- saved_inputs: bfloat16 [32, 256, 3072], P('section', ('tensor', 'dp')), may hold values from -36 to 36
- w_in: bfloat16 [32, 3072, 3072], P('section', None, ('tensor', 'dp')), may hold values from -0.109375 to 0.109375
- w_out: bfloat16 [32, 3072, 3072], P('section', ('tensor', 'dp')), may hold values from -0.078125 to 0.078125
Outputs:
- out_acts: bfloat16 [32, 256, 3072], P('section', ('tensor', 'dp'))
- out_grads: bfloat16 [32, 256, 3072], P('section', ('tensor', 'dp'))
- grad_in: bfloat16 [32, 3072, 3072], P('section', None, ('tensor', 'dp'))
- grad_out: bfloat16 [32, 3072, 3072], P('section', ('tensor', 'dp'))
All inputs are finite; a program needn't handle non-finite values.
Results may differ from a plain program's by a relative error of at most 0.015.
Values may be sent and summed in bfloat16 or wider, within the bound.
A program may use at most 64 MiB of HBM per device.

v0:
```python
import jax
import jax.numpy as jnp
from jax import lax
from jax.sharding import PartitionSpec as P

eps = 1e-05


def shifted(value, axis, steps):
    count = lax.axis_size(axis)
    leading, last = (max(0, -steps), min(count, count - steps))
    return lax.ppermute(value, axis, [(source, source + steps) for source in range(leading, last)])


def swapped(block, axis, bit):
    count = lax.axis_size(axis)
    route = []
    for low in range(count):
        high = low | 1 << bit
        if high != low and high < count:
            route += [(low, high), (high, low)]
    return lax.ppermute(block, axis, route)


def normalize(features):
    inv_scale = lax.rsqrt(jnp.mean(features * features, axis=-1, keepdims=True) + eps)
    return features * inv_scale


def activate(pre_values):
    return jax.nn.gelu(pre_values, approximate=True)


def row_product(left_rows, right_rows):
    return lax.dot_general(
        left_rows, right_rows, (((0,), (0,)), ((), ())), preferred_element_type=jnp.float32
    ).astype(jnp.bfloat16)


def shards(sent_acts, sent_grads, saved_inputs, w_in, w_out):
    section_count = lax.axis_size("section")
    section_half = section_count // 2
    position = lax.axis_index("section")
    within = position % section_half
    upper_half = position // section_half
    lower_side = upper_half == 0
    mirror_bit = section_half.bit_length() - 1
    own_acts = sent_acts[0]
    own_grads = sent_grads[0]
    own_in = w_in[0]
    own_out = w_out[0]
    piece_units = own_in.shape[1]
    keep_start = upper_half * piece_units
    give_start = (1 - upper_half) * piece_units
    arriving = shifted(own_acts, "section", 1)
    returning = shifted(own_grads, "section", -1)
    other_in, other_out = swapped((own_in, own_out), "section", mirror_bit)
    layer_in = jnp.concatenate(
        [jnp.where(lower_side, own_in, other_in), jnp.where(lower_side, other_in, own_in)], axis=1
    )
    layer_out = jnp.concatenate(
        [jnp.where(lower_side, own_out, other_out), jnp.where(lower_side, other_out, own_out)],
        axis=0,
    )
    inputs = jnp.where(within == 0, own_acts, arriving).astype(jnp.float32)
    cotangent = jnp.where(within == section_half - 1, own_grads, returning)
    normed = normalize(inputs).astype(jnp.bfloat16)
    gathered = lax.all_gather(normed, ("tensor", "dp"), axis=0, tiled=True)
    hidden = activate(jnp.dot(gathered, layer_in, preferred_element_type=jnp.float32)).astype(
        jnp.bfloat16
    )
    mixed_sum = lax.psum_scatter(
        jnp.dot(hidden, layer_out, preferred_element_type=jnp.float32).astype(jnp.bfloat16),
        ("tensor", "dp"),
        scatter_dimension=0,
        tiled=True,
    ).astype(jnp.float32)
    out_acts = (inputs + mixed_sum).astype(jnp.bfloat16)
    kept_rows = saved_inputs[0].astype(jnp.float32)
    normed_b, norm_back = jax.vjp(normalize, kept_rows)
    normed_b = normed_b.astype(jnp.bfloat16)
    rows_back, cotangent_all = (
        lax.all_gather(normed_b, ("tensor", "dp"), axis=0, tiled=True),
        lax.all_gather(cotangent, ("tensor", "dp"), axis=0, tiled=True),
    )
    pre_act = jnp.dot(rows_back, layer_in, preferred_element_type=jnp.float32)
    hidden_b, act_back = jax.vjp(activate, pre_act)
    hidden_b = hidden_b.astype(jnp.bfloat16)
    d_hidden = lax.dot_general(
        cotangent_all, layer_out, (((1,), (1,)), ((), ())), preferred_element_type=jnp.float32
    )
    d_pre = act_back(d_hidden)[0].astype(jnp.bfloat16)
    d_normed = lax.psum_scatter(
        lax.dot_general(
            d_pre, layer_in, (((1,), (1,)), ((), ())), preferred_element_type=jnp.float32
        ).astype(jnp.bfloat16),
        ("tensor", "dp"),
        scatter_dimension=0,
        tiled=True,
    ).astype(jnp.float32)
    out_grads = (cotangent.astype(jnp.float32) + norm_back(d_normed)[0]).astype(jnp.bfloat16)
    pre_keep = lax.dynamic_slice_in_dim(d_pre, keep_start, piece_units, 1)
    pre_give = lax.dynamic_slice_in_dim(d_pre, give_start, piece_units, 1)
    hidden_keep = lax.dynamic_slice_in_dim(hidden_b, keep_start, piece_units, 1)
    hidden_give = lax.dynamic_slice_in_dim(hidden_b, give_start, piece_units, 1)
    keep_in = row_product(rows_back, pre_keep)
    keep_out = row_product(hidden_keep, cotangent_all)
    partner_rows, partner_cot, partner_pre, partner_hidden = swapped(
        (rows_back, cotangent_all, pre_give, hidden_give), "section", mirror_bit
    )
    got_in = row_product(partner_rows, partner_pre)
    got_out = row_product(partner_hidden, partner_cot)
    grad_in = (keep_in.astype(jnp.float32) + got_in.astype(jnp.float32)).astype(jnp.bfloat16)
    grad_out = (keep_out.astype(jnp.float32) + got_out.astype(jnp.float32)).astype(jnp.bfloat16)
    return (out_acts[None], out_grads[None], grad_in[None], grad_out[None])


def solution(mesh):
    placed = (
        P("section", ("tensor", "dp"), None),
        P("section", ("tensor", "dp"), None),
        P("section", ("tensor", "dp"), None),
        P("section", None, ("tensor", "dp")),
        P("section", ("tensor", "dp"), None),
    )
    return jax.shard_map(
        shards,
        mesh=mesh,
        in_specs=placed,
        out_specs=(
            P("section", ("tensor", "dp"), None),
            P("section", ("tensor", "dp"), None),
            P("section", None, ("tensor", "dp")),
            P("section", ("tensor", "dp"), None),
        ),
        check_vma=False,
    )
```

profile of v0, /device:TPU:32, one launch (start us, length us, event | category | flops | bytes accessed | tf_op | source)
XLA Modules:
  0.0 308.5 jit_solution(6782026739386649340)
XLA Ops:
  7.2 0.0 all-gather.8.cloned.1.call-start
  7.2 1.1 fusion.33
  8.3 1.6 fusion.34
  10.0 0.0 all-gather.8.cloned.1.call-update
  10.0 0.0 all-gather.6.cloned.1.call-start
  10.0 7.4 %collective-permute-start.3 = (bf16[16,3072]{1,0:T(8,128)(2,1)}, bf16[16,3072]{1,0:T(8,128)(2,1)S(1)}, u32[]{:S(2)}, u32[]{:S(2)}) collective-permute-start(bf16[16,3072]{1,0:T(8,128)(2,1)} %bitcast.37), channel_id=1, source_target_pairs={{16,0},{32,16},{48,32},{64,48},{80,64},{96,80},{112,96},{128,112},... | collective-permute-start | bytes 294920 | tf_op jit(solution)/shard_map/ppermute | solution.py:12
  17.5 2.5 collective-permute-done.3
  19.9 1.5 broadcast_select_fusion.4
  21.5 0.0 all-gather.6.cloned.1.call-update
  21.5 0.0 all-gather.4.cloned.1.call-start
  21.6 1.9 collective-permute-start
  23.5 3.8 %collective-permute-start.2 = (bf16[192,3072]{1,0:T(8,128)(2,1)}, bf16[192,3072]{1,0:T(8,128)(2,1)S(1)}, u32[]{:S(2)}, u32[]{:S(2)}) collective-permute-start(bf16[192,3072]{1,0:T(8,128)(2,1)} %bitcast.35), channel_id=1, source_target_pairs={{0,256},{256,0},{16,272},{272,16},{32,288},{288,32},{48,304},{304,... | collective-permute-start | bytes 3538952 | tf_op jit(solution)/shard_map/ppermute | solution.py:22
  27.3 3.6 %collective-permute-start.1 = (bf16[3072,192]{0,1:T(8,128)(2,1)}, bf16[3072,192]{0,1:T(8,128)(2,1)S(1)}, u32[]{:S(2)}, u32[]{:S(2)}) collective-permute-start(bf16[3072,192]{0,1:T(8,128)(2,1)} %bitcast.36), channel_id=1, source_target_pairs={{0,256},{256,0},{16,272},{272,16},{32,288},{288,32},{48,304},{304,... | collective-permute-start | bytes 3538952 | tf_op jit(solution)/shard_map/ppermute | solution.py:22
  30.9 1.1 fusion.28
  32.0 0.6 copy-done.10
  32.6 0.7 fusion.29
  33.3 0.0 all-gather.4.cloned.1.call-update
  33.4 0.0 reduce-scatter.5.cloned.1.call-start
  33.4 29.9 %collective-permute-done.2 = bf16[192,3072]{1,0:T(8,128)(2,1)S(1)} collective-permute-done((bf16[192,3072]{1,0:T(8,128)(2,1)}, bf16[192,3072]{1,0:T(8,128)(2,1)S(1)}, u32[]{:S(2)}, u32[]{:S(2)}) %collective-permute-start.2) | collective-permute-done | bytes 1179680 | tf_op jit(solution)/shard_map/ppermute | solution.py:22
  63.4 1.6 broadcast_select_fusion.1
  64.9 23.9 %collective-permute-done.1 = bf16[3072,192]{0,1:T(8,128)(2,1)S(1)} collective-permute-done((bf16[3072,192]{0,1:T(8,128)(2,1)}, bf16[3072,192]{0,1:T(8,128)(2,1)S(1)}, u32[]{:S(2)}, u32[]{:S(2)}) %collective-permute-start.1) | collective-permute-done | bytes 1179680 | tf_op jit(solution)/shard_map/ppermute | solution.py:22
  88.8 1.3 broadcast_select_fusion.3
  90.1 4.1 %multiply_convert_fusion = (bf16[256,384]{1,0:T(8,128)(2,1)}, f32[256,384]{1,0:T(8,128)}) fusion(bf16[256,3072]{1,0:T(8,128)(2,1)} %all-gather.8.cloned.1.call-done, bf16[3072,192]{0,1:T(8,128)(2,1)} %get-tuple-element.7, bf16[3072,192]{0,1:T(8,128)(2,1)S(1)} %get-tuple-element.6), kind=kOutput, calls=%fused_computation.43 | convolution fusion | flops 609583104 | bytes 4521984 | tf_op jit(solution)/shard_map/dot_general | solution.py:86
  94.2 7.5 %all-gather.6.cloned.1.call-done = bf16[256,3072]{1,0:T(8,128)(2,1)} async-done(((bf16[16,3072]{1,0:T(8,128)(2,1)}), bf16[256,3072]{1,0:T(8,128)(2,1)}) %all-gather.6.cloned.1.call-update) | async-done | bytes 1572880 | tf_op jit(solution)/shard_map/all_gather | solution.py:84
  101.7 2.7 fusion.19
  104.4 0.7 copy-done.13
  105.1 2.2 convolution_convert_fusion
  107.2 0.0 reduce-scatter.5.cloned.1.call-update
  107.3 0.0 reduce-scatter.3.cloned.1.call-start
  107.3 37.7 %all-gather.4.cloned.1.call-done = bf16[256,3072]{1,0:T(8,128)(2,1)} async-done(((bf16[16,3072]{1,0:T(8,128)(2,1)}), bf16[256,3072]{1,0:T(8,128)(2,1)}) %all-gather.4.cloned.1.call-update) | async-done | bytes 1572880 | tf_op jit(solution)/shard_map/all_gather | solution.py:68
  145.1 5.7 %convolution_convert_fusion.1 = bf16[256,3072]{1,0:T(8,128)(2,1)} fusion(bf16[192,3072]{1,0:T(8,128)(2,1)} %get-tuple-element.9, bf16[192,3072]{1,0:T(8,128)(2,1)S(1)} %copy-done.5, bf16[256,3072]{1,0:T(8,128)(2,1)} %all-gather.4.cloned.1.call-done, bf16[3072,192]{0,1:T(8,128)(2,1)} %get-tuple-element.7, bf16[3072,192]{0,1:T(8,128)(2,1)} %copy-done.7), kind=kOutput, calls=%fused_computation.1 | convolution fusion | flops 1219067904 | bytes 7864320 | tf_op jit(solution)/shard_map/dot_general | solution.py:73
  150.8 0.0 reduce-scatter.3.cloned.1.call-update
  150.8 1.4 copy-done
  152.2 4.6 %collective-permute-start.4 = (bf16[256,3072]{1,0:T(8,128)(2,1)S(1)}, bf16[256,3072]{1,0:T(8,128)(2,1)}, u32[]{:S(2)}, u32[]{:S(2)}) collective-permute-start(bf16[256,3072]{1,0:T(8,128)(2,1)S(1)} %copy-done), channel_id=1, source_target_pairs={{0,256},{256,0},{16,272},{272,16},{32,288},{288,32},{48,304},{304,... | collective-permute-start | bytes 4718600 | tf_op jit(solution)/shard_map/ppermute | solution.py:22
  156.8 2.7 collective-permute-start.7
  159.6 0.1 constant_dynamic-slice_fusion
  159.7 4.6 %collective-permute-start.6 = (bf16[256,192]{1,0:T(8,128)(2,1)S(1)}, bf16[256,192]{1,0:T(8,128)(2,1)S(1)}, u32[]{:S(2)}, u32[]{:S(2)}) collective-permute-start(bf16[256,192]{1,0:T(8,128)(2,1)S(1)} %constant_dynamic-slice_fusion), channel_id=1, source_target_pairs={{0,256},{256,0},{16,272},{272,16},{32,288},{288,32},{48,304},{304,... | collective-permute-start | bytes 294920 | tf_op jit(solution)/shard_map/ppermute | solution.py:22
  164.3 0.1 constant_dynamic-slice_fusion.1
  164.4 2.7 collective-permute-start.5
  167.2 0.6 fusion.7
  167.8 79.5 %collective-permute-done.5 = bf16[256,192]{1,0:T(8,128)(2,1)S(1)} collective-permute-done((bf16[256,192]{1,0:T(8,128)(2,1)S(1)}, bf16[256,192]{1,0:T(8,128)(2,1)S(1)}, u32[]{:S(2)}, u32[]{:S(2)}) %collective-permute-start.5) | collective-permute-done | bytes 98336 | tf_op jit(solution)/shard_map/ppermute | solution.py:22
  247.2 3.0 fusion.8
  250.2 1.9 fusion
  252.2 1.6 fusion.9
  253.8 1.0 fusion.35
  254.9 43.8 %reduce-scatter.3.cloned.1.call-done = bf16[16,3072]{1,0:T(8,128)(2,1)} async-done(((bf16[256,3072]{1,0:T(8,128)(2,1)}), bf16[16,3072]{1,0:T(8,128)(2,1)}) %reduce-scatter.3.cloned.1.call-update) | async-done | bytes 98320 | tf_op jit(solution)/shard_map/reduce_scatter | solution.py:72
  298.7 1.6 fusion.43
  300.3 1.7 fusion.42
  (36 shorter events, 0.1 us)
Async XLA Ops:
  7.2 56.2 %copy-start.3 = (bf16[1,192,3072]{2,1,0:T(8,128)(2,1)S(1)}, bf16[1,192,3072]{2,1,0:T(8,128)(2,1)}, u32[]{:S(2)}) copy-start(bf16[1,192,3072]{2,1,0:T(8,128)(2,1)} %param.9) | copy-start | bytes 3538948
  7.2 82.9 %all-gather.8.cloned.1.call-start = ((), (), s32[]{:S(2)}) async-start(), calls=%async_computation.5 | async-start | bytes 1671168 | tf_op jit(solution)/shard_map/all_gather | solution.py:83
  10.0 91.7 %all-gather.6.cloned.1.call-start = ((), (), s32[]{:S(2)}) async-start(), calls=%async_computation.4 | async-start | bytes 1671168 | tf_op jit(solution)/shard_map/all_gather | solution.py:84
  10.0 9.9 %collective-permute-start.3 = (bf16[16,3072]{1,0:T(8,128)(2,1)}, bf16[16,3072]{1,0:T(8,128)(2,1)S(1)}, u32[]{:S(2)}, u32[]{:S(2)}) collective-permute-start(bf16[16,3072]{1,0:T(8,128)(2,1)} %bitcast.37), channel_id=1, source_target_pairs={{16,0},{32,16},{48,32},{64,48},{80,64},{96,80},{112,96},{128,112},... | collective-permute-start | bytes 294920 | tf_op jit(solution)/shard_map/ppermute | solution.py:12
  21.5 123.5 %all-gather.4.cloned.1.call-start = ((), (), s32[]{:S(2)}) async-start(), calls=%async_computation.2 | async-start | bytes 1671168 | tf_op jit(solution)/shard_map/all_gather | solution.py:68
  21.6 9.3 %collective-permute-start = (bf16[16,3072]{1,0:T(8,128)(2,1)}, bf16[16,3072]{1,0:T(8,128)(2,1)}, u32[]{:S(2)}, u32[]{:S(2)}) collective-permute-start(bf16[16,3072]{1,0:T(8,128)(2,1)} %bitcast.38), channel_id=1, source_target_pairs={{0,16},{16,32},{32,48},{48,64},{64,80},{80,96},{96,112},{112,128},... | collective-permute-start | bytes 294920 | tf_op jit(solution)/shard_map/ppermute | solution.py:12
  23.5 39.9 %collective-permute-start.2 = (bf16[192,3072]{1,0:T(8,128)(2,1)}, bf16[192,3072]{1,0:T(8,128)(2,1)S(1)}, u32[]{:S(2)}, u32[]{:S(2)}) collective-permute-start(bf16[192,3072]{1,0:T(8,128)(2,1)} %bitcast.35), channel_id=1, source_target_pairs={{0,256},{256,0},{16,272},{272,16},{32,288},{288,32},{48,304},{304,... | collective-permute-start | bytes 3538952 | tf_op jit(solution)/shard_map/ppermute | solution.py:22
  27.3 61.6 %collective-permute-start.1 = (bf16[3072,192]{0,1:T(8,128)(2,1)}, bf16[3072,192]{0,1:T(8,128)(2,1)S(1)}, u32[]{:S(2)}, u32[]{:S(2)}) collective-permute-start(bf16[3072,192]{0,1:T(8,128)(2,1)} %bitcast.36), channel_id=1, source_target_pairs={{0,256},{256,0},{16,272},{272,16},{32,288},{288,32},{48,304},{304,... | collective-permute-start | bytes 3538952 | tf_op jit(solution)/shard_map/ppermute | solution.py:22
  32.0 0.6 copy-start.10
  33.4 220.5 %reduce-scatter.5.cloned.1.call-start = ((), (), s32[]{:S(2)}) async-start(), calls=%async_computation.6 | async-start | bytes 1671168 | tf_op jit(solution)/shard_map/reduce_scatter | solution.py:93
  33.4 55.4 %copy-start.4 = (bf16[1,3072,192]{1,2,0:T(8,128)(2,1)S(1)}, bf16[1,3072,192]{1,2,0:T(8,128)(2,1)}, u32[]{:S(2)}) copy-start(bf16[1,3072,192]{1,2,0:T(8,128)(2,1)} %param.8) | copy-start | bytes 3538948
  90.1 14.3 %copy-start.7 = (bf16[3072,192]{0,1:T(8,128)(2,1)}, bf16[3072,192]{0,1:T(8,128)(2,1)S(1)}, u32[]{:S(2)}) copy-start(bf16[3072,192]{0,1:T(8,128)(2,1)S(1)} %get-tuple-element.6) | copy-start | bytes 3538948
  90.1 11.6 %copy-start.5 = (bf16[192,3072]{1,0:T(8,128)(2,1)S(1)}, bf16[192,3072]{1,0:T(8,128)(2,1)}, u32[]{:S(2)}) copy-start(bf16[192,3072]{1,0:T(8,128)(2,1)} %get-tuple-element.8) | copy-start | bytes 3538948
  90.1 11.6 %copy-start.6 = (bf16[192,3072]{1,0:T(8,128)(2,1)S(1)}, bf16[192,3072]{1,0:T(8,128)(2,1)}, u32[]{:S(2)}) copy-start(bf16[192,3072]{1,0:T(8,128)(2,1)} %get-tuple-element.9) | copy-start | bytes 3538948
  101.7 3.4 %copy-start.8 = (bf16[3072,192]{0,1:T(8,128)(2,1)S(1)}, bf16[3072,192]{0,1:T(8,128)(2,1)}, u32[]{:S(2)}) copy-start(bf16[3072,192]{0,1:T(8,128)(2,1)} %get-tuple-element.7) | copy-start | bytes 3538948
  104.4 0.7 copy-start.13
  107.3 191.5 %reduce-scatter.3.cloned.1.call-start = ((), (), s32[]{:S(2)}) async-start(), calls=%async_computation.3 | async-start | bytes 1671168 | tf_op jit(solution)/shard_map/reduce_scatter | solution.py:72
  145.0 11.8 %copy-start.2 = (bf16[256,3072]{1,0:T(8,128)(2,1)S(1)}, bf16[256,3072]{1,0:T(8,128)(2,1)}, u32[]{:S(2)}) copy-start(bf16[256,3072]{1,0:T(8,128)(2,1)} %all-gather.6.cloned.1.call-done) | copy-start | bytes 4718596
  145.0 14.5 %copy-start.12 = (bf16[256,384]{1,0:T(8,128)(2,1)S(1)}, bf16[256,384]{1,0:T(8,128)(2,1)}, u32[]{:S(2)}) copy-start(bf16[256,384]{1,0:T(8,128)(2,1)} %get-tuple-element.10) | copy-start | bytes 589828
  150.8 1.4 copy-start
  150.8 13.5 %copy-start.14 = (bf16[256,384]{1,0:T(8,128)(2,1)S(1)}, bf16[256,384]{1,0:T(8,128)(2,1)}, u32[]{:S(2)}) copy-start(bf16[256,384]{1,0:T(8,128)(2,1)} %copy-done.13) | copy-start | bytes 589828
  152.2 95.0 %collective-permute-start.4 = (bf16[256,3072]{1,0:T(8,128)(2,1)S(1)}, bf16[256,3072]{1,0:T(8,128)(2,1)}, u32[]{:S(2)}, u32[]{:S(2)}) collective-permute-start(bf16[256,3072]{1,0:T(8,128)(2,1)S(1)} %copy-done), channel_id=1, source_target_pairs={{0,256},{256,0},{16,272},{272,16},{32,288},{288,32},{48,304},{304,... | collective-permute-start | bytes 4718600 | tf_op jit(solution)/shard_map/ppermute | solution.py:22
  156.8 93.4 %collective-permute-start.7 = (bf16[256,3072]{1,0:T(8,128)(2,1)S(1)}, bf16[256,3072]{1,0:T(8,128)(2,1)}, u32[]{:S(2)}, u32[]{:S(2)}) collective-permute-start(bf16[256,3072]{1,0:T(8,128)(2,1)S(1)} %copy-done.2), channel_id=1, source_target_pairs={{0,256},{256,0},{16,272},{272,16},{32,288},{288,32},{48,304},{304,... | collective-permute-start | bytes 4718600 | tf_op jit(solution)/shard_map/ppermute | solution.py:22
  159.7 90.5 %collective-permute-start.6 = (bf16[256,192]{1,0:T(8,128)(2,1)S(1)}, bf16[256,192]{1,0:T(8,128)(2,1)S(1)}, u32[]{:S(2)}, u32[]{:S(2)}) collective-permute-start(bf16[256,192]{1,0:T(8,128)(2,1)S(1)} %constant_dynamic-slice_fusion), channel_id=1, source_target_pairs={{0,256},{256,0},{16,272},{272,16},{32,288},{288,32},{48,304},{304,... | collective-permute-start | bytes 294920 | tf_op jit(solution)/shard_map/ppermute | solution.py:22
  164.4 82.8 %collective-permute-start.5 = (bf16[256,192]{1,0:T(8,128)(2,1)S(1)}, bf16[256,192]{1,0:T(8,128)(2,1)S(1)}, u32[]{:S(2)}, u32[]{:S(2)}) collective-permute-start(bf16[256,192]{1,0:T(8,128)(2,1)S(1)} %constant_dynamic-slice_fusion.1), channel_id=1, source_target_pairs={{0,256},{256,0},{16,272},{272,16},{32,288},{288,32},{48,304},{304,... | collective-permute-start | bytes 294920 | tf_op jit(solution)/shard_map/ppermute | solution.py:22
  252.2 1.7 copy-start.1
  252.2 46.6 %copy-start.11 = (bf16[16,3072]{1,0:T(8,128)(2,1)S(1)}, bf16[16,3072]{1,0:T(8,128)(2,1)}, u32[]{:S(2)}) copy-start(bf16[16,3072]{1,0:T(8,128)(2,1)} %copy-done.10) | copy-start | bytes 294916
  252.2 48.1 %copy-start.9 = (bf16[16,3072]{1,0:T(8,128)(2,1)S(1)}, bf16[16,3072]{1,0:T(8,128)(2,1)}, u32[]{:S(2)}) copy-start(bf16[16,3072]{1,0:T(8,128)(2,1)} %broadcast_select_fusion.4) | copy-start | bytes 294916
Sparse Core Ops, SparseCore 0:
  10.2 47.0 all-gather.7
  59.3 42.2 all-gather.5
  104.4 40.5 all-gather.3
  147.7 77.3 reduce-scatter.4
  228.0 70.6 reduce-scatter.2
where the time goes:
time: 309 us; the launch traced here: 308 us
  waiting for transfers between devices  225 us (73%)
  starting transfers between devices  31.6 us (10%)
  matrix products  21.8 us (7%)
  between operations  14 us (5%)
  other arithmetic  13.2 us (4%)
    ppermute x6, waiting for transfers between devices, swapped(): return lax.ppermute(block, axis, route)  133 us
    reduce_scatter x1, waiting for transfers between devices, shards(): lax.psum_scatter(jnp.dot(hidden, layer_out, preferred_element_type=jnp.fl...  43.8 us
    all_gather x1, waiting for transfers between devices, shards(): gathered = lax.all_gather(normed, ('tensor', 'dp'), axis=0, tiled=True)  37.7 us
    ppermute x6, starting transfers between devices, swapped(): return lax.ppermute(block, axis, route)  22 us
    ppermute x2, starting transfers between devices, shifted(): lax.ppermute(value, axis, [(source, source + steps) for source in range(l...  9.32 us
    all_gather x1, waiting for transfers between devices, shards(): lax.all_gather(cotangent, ('tensor', 'dp'), axis=0, tiled=True)  7.49 us
    dot_general x4, matrix products, row_product(): lax.dot_general(left_rows, right_rows, (((0,), (0,)), ((), ())), preferre...  7.15 us
  transfers between devices with their start and end apart: 13, of which 7 were waited for; matrix products, arithmetic and copies ran while one was open for 9% of the time, Pallas kernels for 0%

commit v1 on v0

v1 whole, which is shorter than its diff:
```python
import functools

import jax
import jax.numpy as jnp
from jax import lax
from jax.experimental import pallas as pl
from jax.experimental.pallas import tpu as pltpu
from jax.sharding import PartitionSpec as P

MESH = pl.DeviceIdType.MESH
F32, BF16 = jnp.float32, jnp.bfloat16
EPS = 1e-05
NB, CT, NF = 0, 1, 2
BWD, FWD = 0, 1
GELU_A, GELU_B = 0.7978845608028654, 0.044715


def inv_rms(values):
    return lax.rsqrt(jnp.mean(values * values, axis=-1, keepdims=True) + EPS)


def gelu(v):
    return 0.5 * v * (1.0 + jnp.tanh(GELU_A * (v + GELU_B * (v * v * v))))


def gelu_and_slope(v):
    square = v * v
    t = jnp.tanh(GELU_A * (v + GELU_B * (v * square)))
    value = 0.5 * v * (1.0 + t)
    slope = 0.5 * (1.0 + t) + 0.5 * v * (1.0 - t * t) * (GELU_A * (1.0 + 3.0 * GELU_B * square))
    return value, slope


def nn(a, b):
    return jnp.dot(a, b, preferred_element_type=F32)


def nt(a, b):
    return lax.dot_general(a, b, (((1,), (1,)), ((), ())), preferred_element_type=F32)


def tn(a, b):
    return lax.dot_general(a, b, (((0,), (0,)), ((), ())), preferred_element_type=F32)


def kernel(
    n_z, acts, grads, saved, w_in, w_out, o_acts, o_grads, o_gin, o_gout,
    tok, ag, win, wout, part, r1, r2, r3, r4, q, hid, dpre, slope, gin_s, gin_r, gout_s, gout_r, gin_o, gout_o,
    loc_sem, ag_send, ag_recv, rs_send, rs_recv, ex_send, ex_recv,
):
    sec, y, dp = lax.axis_index("section"), lax.axis_index("tensor"), lax.axis_index("dp")
    z = lax.rem(sec, n_z)
    x_hi = sec // n_z
    x = 2 * x_hi + dp // 2
    core = lax.rem(dp, 2)
    D = ag.shape[-1]
    H, Q = D // 2, D // 4
    tokens = 16 * ag.shape[3]

    def at(dy, dx):
        return lax.rem(y + dy + 4, 4), lax.rem(x + dx + 4, 4)

    def chip(dy, dx):
        yy, xx = at(dy, dx)
        return ((xx // 2) * n_z + z, yy, 2 * lax.rem(xx, 2) + core)

    def plane(dz):
        return (x_hi * n_z + lax.rem(z + dz + n_z, n_z), y, dp)

    sibling = (sec, y, dp + 1 - 2 * core)

    sent = []

    def send(src, dst, ssem, rsem, dev):
        copy = pltpu.make_async_remote_copy(
            src_ref=src, dst_ref=dst, send_sem=ssem, recv_sem=rsem, device_id=dev, device_id_type=MESH
        )
        copy.start()
        sent.append(copy)
        return copy

    def local(src, dst, i):
        copy = pltpu.make_async_copy(src, dst, loc_sem.at[i])
        copy.start()
        return copy

    c_saved = local(saved.at[0], tok.at[0], 0)
    c_acts = local(acts.at[0], tok.at[1], 1)
    c_grads = local(grads.at[0], tok.at[2], 2)
    c_win = local(w_in.at[0], win.at[0], 3)
    c_wout = local(w_out.at[0], wout.at[0], 4)

    partners = [chip(0, 1), chip(0, -1), chip(1, 0), chip(-1, 0), plane(1), plane(-1), sibling]
    barrier = pltpu.get_barrier_semaphore()
    for dev in partners:
        pl.semaphore_signal(barrier, inc=1, device_id=dev, device_id_type=MESH)
    pl.semaphore_wait(barrier, len(partners))

    x_acts = send(acts.at[0], tok.at[3], ex_send.at[0], ex_recv.at[0], plane(1))
    x_grads = send(grads.at[0], tok.at[4], ex_send.at[1], ex_recv.at[1], plane(-1))
    x_win = send(w_in.at[0], win.at[1], ex_send.at[2], ex_recv.at[2], sibling)
    x_wout = send(w_out.at[0], wout.at[1], ex_send.at[3], ex_recv.at[3], sibling)

    def cols(h, part_no=None):
        if part_no is None:
            return pl.ds(h * H, H)
        return pl.ds(h * H + part_no * Q, Q)

    def first(h, d):
        return (0, d) if h == 0 else (d, 0)

    def second(h, d):
        return (d, 0) if h == 0 else (0, d)

    def slot(h, df, ds):
        return at(ds, df) if h == 0 else at(df, ds)

    msgs = {}

    def ag_send_msg(k, h, m, df, ds, sub, dev):
        yy, xx = slot(h, df, ds)
        ref = ag.at[k, yy, xx, :, cols(h, sub)]
        msgs[k, h, m] = send(ref, ref, ag_send.at[k, h, m], ag_recv.at[k, h, m], chip(*dev))

    J = (0, -1, 1, 2)

    def ag0(k, h):
        ag_send_msg(k, h, 0, 0, 0, None, first(h, 1))
        ag_send_msg(k, h, 1, 0, 0, None, first(h, -1))
        ag_send_msg(k, h, 4, 0, 0, None, second(h, 1))
        ag_send_msg(k, h, 5, 0, 0, None, second(h, -1))

    def ag1(k, h):
        for m, d in ((0, -1), (1, 1)):
            msgs[k, h, m].wait_recv()
            ag_send_msg(k, h, 2 + m, d, 0, m, first(h, -d))
            j = J.index(d)
            ag_send_msg(k, h, 4 + 2 * j, d, 0, None, second(h, 1))
            ag_send_msg(k, h, 5 + 2 * j, d, 0, None, second(h, -1))

    def ag_forward(k, h, j):
        for m, d in ((0, -1), (1, 1)):
            msgs[k, h, 4 + 2 * j + m].wait_recv()
            ag_send_msg(k, h, 12 + 2 * j + m, J[j], d, m, second(h, -d))

    def ag2(k, h):
        ag_forward(k, h, 0)

    def ag3(k, h):
        msgs[k, h, 2].wait_recv()
        msgs[k, h, 3].wait_recv()
        ag_send_msg(k, h, 10, 2, 0, None, second(h, 1))
        ag_send_msg(k, h, 11, 2, 0, None, second(h, -1))

    def ag4(k, h):
        ag_forward(k, h, 1)
        ag_forward(k, h, 2)

    def ag5(k, h):
        ag_forward(k, h, 3)

    def ag6(k, h):
        for m in range(12, 20):
            msgs[k, h, m].wait_recv()

    ag_stages = (ag0, ag1, ag2, ag3, ag4, ag5, ag6)

    def gather(k, stage):
        for h in range(2):
            ag_stages[stage](k, h)

    def row(ref, h, d, csl):
        if h == 0:
            return ref.at[at(d, 0)[0], :, :, csl]
        return ref.at[:, at(0, d)[1], :, csl]

    rmsgs = {}

    def rs_send_msg(r, h, m, src, dst, dev):
        rmsgs[r, h, m] = send(src, dst, rs_send.at[r, h, m], rs_recv.at[r, h, m], chip(*dev))

    def rs0(r, h):
        p = part.at[r]
        for m, d in ((0, 1), (1, -1)):
            rs_send_msg(r, h, m, row(p, h, 2, cols(h, m)), r1.at[r, h, m], second(h, d))
        for m, d in ((0, 1), (1, -1)):
            rs_send_msg(
                r, h, 2 + m, row(p, h, d, cols(h, 1 - m)), r2.at[r, h, m, :, :, pl.ds((1 - m) * Q, Q)], second(h, d)
            )

    def rs1(r, h):
        p = part.at[r]
        for m, d in ((0, 1), (1, -1)):
            rmsgs[r, h, m].wait_recv()
            near = row(p, h, d, cols(h, m))
            near[...] = (near[...].astype(F32) + r1[r, h, m].astype(F32)).astype(BF16)
            rs_send_msg(r, h, 4 + m, near, r2.at[r, h, m, :, :, pl.ds(m * Q, Q)], second(h, d))

    def rs2(r, h):
        p = part.at[r]
        for m in range(2, 6):
            rmsgs[r, h, m].wait_recv()
        own = row(p, h, 0, cols(h))
        q[r, h] = (own[...].astype(F32) + r2[r, h, 0].astype(F32) + r2[r, h, 1].astype(F32)).astype(BF16)

        def place(d):
            return at(0, d)[1] if h == 0 else at(d, 0)[0]

        for m, d in ((0, 1), (1, -1)):
            rs_send_msg(
                r, h, 6 + m, q.at[r, h, place(2), :, pl.ds(m * Q, Q)], r3.at[r, h, m], first(h, d)
            )
        for m, d in ((0, 1), (1, -1)):
            rs_send_msg(
                r, h, 8 + m, q.at[r, h, place(d), :, pl.ds((1 - m) * Q, Q)],
                r4.at[r, h, m, :, pl.ds((1 - m) * Q, Q)], first(h, d),
            )

    def rs3(r, h):
        def place(d):
            return at(0, d)[1] if h == 0 else at(d, 0)[0]

        for m, d in ((0, 1), (1, -1)):
            rmsgs[r, h, 6 + m].wait_recv()
            near = q.at[r, h, place(d), :, pl.ds(m * Q, Q)]
            near[...] = (near[...].astype(F32) + r3[r, h, m].astype(F32)).astype(BF16)
            rs_send_msg(r, h, 10 + m, near, r4.at[r, h, m, :, pl.ds(m * Q, Q)], first(h, d))

    def rs4(r, h):
        for m in range(8, 12):
            rmsgs[r, h, m].wait_recv()
        place = x if h == 0 else y
        return q[r, h, place].astype(F32) + r4[r, h, 0].astype(F32) + r4[r, h, 1].astype(F32)

    rs_stages = (rs0, rs1, rs2, rs3)

    def scatter(r, stage):
        for h in range(2):
            rs_stages[stage](r, h)

    def rows(k):
        return ag[k].reshape(tokens, D)

    c_saved.wait()
    kept = tok[0].astype(F32)
    ag[NB, y, x] = (kept * inv_rms(kept)).astype(BF16)
    gather(NB, 0)
    c_acts.wait()
    c_grads.wait()
    x_grads.wait_recv()
    ag[CT, y, x] = jnp.where(z == n_z - 1, tok[2], tok[4])
    x_acts.wait_recv()
    tok[1] = jnp.where(z == 0, tok[1], tok[3])
    inputs = tok[1].astype(F32)
    ag[NF, y, x] = (inputs * inv_rms(inputs)).astype(BF16)
    gather(NB, 1)
    gather(NB, 2)
    gather(NB, 3)
    gather(CT, 0)
    gather(NB, 4)
    gather(CT, 1)
    gather(NB, 5)
    gather(CT, 2)
    gather(CT, 3)
    gather(NB, 6)
    gather(NF, 0)
    gather(CT, 4)
    c_win.wait()
    x_win.wait_recv()
    for c in range(2):
        value, grad = gelu_and_slope(nn(rows(NB), win[c]))
        hid[c] = value.astype(BF16)
        slope[c] = grad
    gather(NF, 1)
    gather(CT, 5)
    gather(NF, 2)
    gather(NF, 3)
    gather(CT, 6)
    gather(NF, 4)
    c_wout.wait()
    x_wout.wait_recv()
    for c in range(2):
        dpre[c] = (nt(rows(CT), wout[c]) * slope[c]).astype(BF16)
    gather(NF, 5)
    for h in range(2):
        for s in range(2):
            csl = cols(h, s)
            part[BWD, :, :, :, csl] = (
                (nt(dpre[0], win[0, csl, :]) + nt(dpre[1], win[1, csl, :])).astype(BF16).reshape(4, 4, 16, Q)
            )
        rs0(BWD, h)
    gather(NF, 6)
    for c in range(2):
        hid_f = gelu(nn(rows(NF), win[c])).astype(BF16)
        slope[c] = hid_f.astype(F32)
    scatter(BWD, 1)
    for h in range(2):
        for s in range(2):
            csl = cols(h, s)
            part[FWD, :, :, :, csl] = (
                (nn(slope[0].astype(BF16), wout[0, :, csl]) + nn(slope[1].astype(BF16), wout[1, :, csl]))
                .astype(BF16).reshape(4, 4, 16, Q)
            )
        rs0(FWD, h)
    scatter(BWD, 2)
    gin_s[...] = tn(rows(NB), dpre[1]).astype(BF16)
    x_gin = send(gin_s, gin_r, ex_send.at[4], ex_recv.at[4], sibling)
    scatter(BWD, 3)
    scatter(FWD, 1)
    gout_s[...] = tn(hid[1], rows(CT)).astype(BF16)
    x_gout = send(gout_s, gout_r, ex_send.at[5], ex_recv.at[5], sibling)
    scatter(FWD, 2)
    gin_o[...] = tn(rows(NB), dpre[0]).astype(BF16)
    gout_o[...] = tn(hid[0], rows(CT)).astype(BF16)
    scatter(FWD, 3)
    x_gin.wait_recv()
    gin_o[...] = (gin_o[...].astype(F32) + gin_r[...].astype(F32)).astype(BF16)
    out_gin = pltpu.make_async_copy(gin_o, o_gin.at[0], loc_sem.at[5])
    out_gin.start()
    x_gout.wait_recv()
    gout_o[...] = (gout_o[...].astype(F32) + gout_r[...].astype(F32)).astype(BF16)
    out_gout = pltpu.make_async_copy(gout_o, o_gout.at[0], loc_sem.at[6])
    out_gout.start()

    d_normed = jnp.concatenate([rs4(BWD, 0), rs4(BWD, 1)], axis=-1)
    kept = tok[0].astype(F32)
    scale = inv_rms(kept)
    inner = jnp.mean(d_normed * kept, axis=-1, keepdims=True)
    back = scale * d_normed - kept * (scale * scale * scale * inner)
    o_grads[0] = (ag[CT, y, x].astype(F32) + back).astype(BF16)
    o_acts[0] = (tok[1].astype(F32) + jnp.concatenate([rs4(FWD, 0), rs4(FWD, 1)], axis=-1)).astype(BF16)
    out_gin.wait()
    out_gout.wait()
    for copy in sent:
        copy.wait_send()


def shards(n_z, acts, grads, saved, w_in, w_out):
    _, T, D = acts.shape
    U = w_in.shape[2]
    H, Q = D // 2, D // 4
    vmem = pltpu.VMEM
    sem = pltpu.SemaphoreType.DMA
    anywhere = pl.BlockSpec(memory_space=pl.ANY)
    whole = pl.BlockSpec(memory_space=pltpu.VMEM)
    tokens = 16 * T
    return pl.pallas_call(
        functools.partial(kernel, n_z),
        out_shape=(
            jax.ShapeDtypeStruct(acts.shape, BF16),
            jax.ShapeDtypeStruct(acts.shape, BF16),
            jax.ShapeDtypeStruct(w_in.shape, BF16),
            jax.ShapeDtypeStruct(w_out.shape, BF16),
        ),
        in_specs=[anywhere] * 5,
        out_specs=(whole, whole, anywhere, anywhere),
        scratch_shapes=[
            vmem((5, T, D), BF16),
            vmem((3, 4, 4, T, D), BF16),
            vmem((2, D, U), BF16),
            vmem((2, U, D), BF16),
            vmem((2, 4, 4, T, D), BF16),
            vmem((2, 2, 2, 4, T, Q), BF16),
            vmem((2, 2, 2, 4, T, H), BF16),
            vmem((2, 2, 2, T, Q), BF16),
            vmem((2, 2, 2, T, H), BF16),
            vmem((2, 2, 4, T, H), BF16),
            vmem((2, tokens, U), BF16),
            vmem((2, tokens, U), BF16),
            vmem((2, tokens, U), F32),
            vmem((D, U), BF16),
            vmem((D, U), BF16),
            vmem((U, D), BF16),
            vmem((U, D), BF16),
            vmem((D, U), BF16),
            vmem((U, D), BF16),
            sem((7,)),
            sem((3, 2, 20)),
            sem((3, 2, 20)),
            sem((2, 2, 12)),
            sem((2, 2, 12)),
            sem((6,)),
            sem((6,)),
        ],
        compiler_params=pltpu.CompilerParams(
            collective_id=0, has_side_effects=True, vmem_limit_bytes=56 * 1024 * 1024
        ),
    )(acts, grads, saved, w_in, w_out)


def solution(mesh):
    rows_split = P("section", ("tensor", "dp"), None)
    columns_split = P("section", None, ("tensor", "dp"))
    return jax.shard_map(
        functools.partial(shards, mesh.shape["section"] // 2),
        mesh=mesh,
        in_specs=(rows_split, rows_split, rows_split, columns_split, rows_split),
        out_specs=(rows_split, rows_split, columns_split, rows_split),
        check_vma=False,
    )
```

time: 309 us -> 83.5 us (0.27)
  the two profiles are of different devices: /device:TPU:32 before, /device:TPU:8 now
where the time goes in v1:
time: 83.5 us; the launch traced here: 83.4 us
  Pallas kernels  75.3 us (90%)
  local copies, waits for them, and re-layouts  7.41 us (9%)
    pallas_call x1, Pallas kernels, shards(): pl.pallas_call(functools.partial(kernel, n_z), out_shape=(jax.ShapeDtypeS...  75.3 us
    unnamed x10, local copies, waits for them, and re-layouts  4.82 us
    pallas_call x1, local copies, waits for them, and re-layouts, shards(): pl.pallas_call(functools.partial(kernel, n_z), out_shape=(jax.ShapeDtypeS...  2.59 us

profile of v1, /device:TPU:8, one launch (start us, length us, event | category | flops | bytes accessed | tf_op | source)
XLA Modules:
  0.0 83.4 jit_solution(11051343900299311178)
XLA Ops:
  0.6 2.5 %copy.9.w_in = bf16[1,3072,192]{2,1,0:T(8,128)(2,1)} copy(bf16[1,3072,192]{1,2,0:T(8,128)(2,1)} %param.8) | data formatting | bytes 2359296 | tf_op args[3]
  3.1 75.3 %shard_map.84 = (bf16[1,16,3072]{2,1,0:T(8,128)(2,1)}, bf16[1,16,3072]{2,1,0:T(8,128)(2,1)}, bf16[1,3072,192]{2,1,0:T(8,128)(2,1)}, bf16[1,192,3072]{2,1,0:T(8,128)(2,1)}) custom-call(bf16[1,16,3072]{2,1,0:T(8,128)(2,1)} %acts.1, bf16[1,16,3072]{2,1,0:T(8,128)(2,1)} %grads.1, bf16[1,16,3072]{2,1,0:T(8,128)(2,1)} %saved.1, bf16[1,3072,192]{2,1,0:T(8,128)(2,1)} %copy.9.w_in, ...), custom_call_target="tpu_custom_call" | custom-call | tf_op jit(solution)/shard_map/pallas_call | solution.py:347
  78.4 0.0 copy-start.2
  78.4 0.0 copy-start.1
  78.5 0.0 copy-start
  78.5 2.6 %copy.10 = bf16[1,3072,192]{1,2,0:T(8,128)(2,1)} copy(bf16[1,3072,192]{2,1,0:T(8,128)(2,1)} %get-tuple-element.6) | data formatting | bytes 2359296 | tf_op jit(solution)/shard_map/pallas_call | solution.py:347
  81.1 0.0 copy-done.2
  81.1 0.6 copy.14
  81.7 0.0 copy-done.1
  81.7 0.6 copy.15
  82.3 0.0 copy-done
  82.3 1.0 %copy.16 = bf16[1,192,3072]{2,1,0:T(8,128)(2,1)} copy(bf16[1,192,3072]{2,1,0:T(8,128)(2,1)S(1)} %copy-done) | data formatting | bytes 2359296
Async XLA Ops:
  78.4 2.6 %copy-start.2 = (bf16[1,16,3072]{2,1,0:T(8,128)(2,1)S(1)}, bf16[1,16,3072]{2,1,0:T(8,128)(2,1)}, u32[]{:S(2)}) copy-start(bf16[1,16,3072]{2,1,0:T(8,128)(2,1)} %get-tuple-element.12) | copy-start | bytes 294916
  78.4 3.3 %copy-start.1 = (bf16[1,16,3072]{2,1,0:T(8,128)(2,1)S(1)}, bf16[1,16,3072]{2,1,0:T(8,128)(2,1)}, u32[]{:S(2)}) copy-start(bf16[1,16,3072]{2,1,0:T(8,128)(2,1)} %get-tuple-element.13) | copy-start | bytes 294916
  78.5 3.9 %copy-start = (bf16[1,192,3072]{2,1,0:T(8,128)(2,1)S(1)}, bf16[1,192,3072]{2,1,0:T(8,128)(2,1)}, u32[]{:S(2)}) copy-start(bf16[1,192,3072]{2,1,0:T(8,128)(2,1)} %get-tuple-element.15) | copy-start | bytes 3538948

commit v2 on v1

--- a/solution.py
+++ b/solution.py
@@ -45,7 +45,7 @@
 
 def kernel(
     n_z, acts, grads, saved, w_in, w_out, o_acts, o_grads, o_gin, o_gout,
-    tok, ag, win, wout, part, r1, r2, r3, r4, q, hid, dpre, slope, gin_s, gin_r, gout_s, gout_r, gin_o, gout_o,
+    tok, ag, win, wout, part, r1, r2, r3, r4, q, hid, fwd_hid, dpre, slope, gin_s, gin_r, gout_s, gout_r,
     loc_sem, ag_send, ag_recv, rs_send, rs_recv, ex_send, ex_recv,
 ):
     sec, y, dp = lax.axis_index("section"), lax.axis_index("tensor"), lax.axis_index("dp")
@@ -98,9 +98,6 @@
 
     x_acts = send(acts.at[0], tok.at[3], ex_send.at[0], ex_recv.at[0], plane(1))
     x_grads = send(grads.at[0], tok.at[4], ex_send.at[1], ex_recv.at[1], plane(-1))
-    x_win = send(w_in.at[0], win.at[1], ex_send.at[2], ex_recv.at[2], sibling)
-    x_wout = send(w_out.at[0], wout.at[1], ex_send.at[3], ex_recv.at[3], sibling)
-
     def cols(h, part_no=None):
         if part_no is None:
             return pl.ds(h * H, H)
@@ -241,123 +238,172 @@
     def rows(k):
         return ag[k].reshape(tokens, D)
 
-    c_saved.wait()
-    kept = tok[0].astype(F32)
-    ag[NB, y, x] = (kept * inv_rms(kept)).astype(BF16)
-    gather(NB, 0)
-    c_acts.wait()
-    c_grads.wait()
-    x_grads.wait_recv()
-    ag[CT, y, x] = jnp.where(z == n_z - 1, tok[2], tok[4])
-    x_acts.wait_recv()
-    tok[1] = jnp.where(z == 0, tok[1], tok[3])
-    inputs = tok[1].astype(F32)
-    ag[NF, y, x] = (inputs * inv_rms(inputs)).astype(BF16)
-    gather(NB, 1)
-    gather(NB, 2)
-    gather(NB, 3)
-    gather(CT, 0)
-    gather(NB, 4)
-    gather(CT, 1)
-    gather(NB, 5)
-    gather(CT, 2)
-    gather(CT, 3)
-    gather(NB, 6)
-    gather(NF, 0)
-    gather(CT, 4)
-    c_win.wait()
-    x_win.wait_recv()
-    for c in range(2):
-        value, grad = gelu_and_slope(nn(rows(NB), win[c]))
-        hid[c] = value.astype(BF16)
-        slope[c] = grad
-    gather(NF, 1)
-    gather(CT, 5)
-    gather(NF, 2)
-    gather(NF, 3)
-    gather(CT, 6)
-    gather(NF, 4)
-    c_wout.wait()
-    x_wout.wait_recv()
-    for c in range(2):
-        dpre[c] = (nt(rows(CT), wout[c]) * slope[c]).astype(BF16)
-    gather(NF, 5)
-    for h in range(2):
+    def prep_nb():
+        c_saved.wait()
+        kept = tok[0].astype(F32)
+        ag[NB, y, x] = (kept * inv_rms(kept)).astype(BF16)
+
+    def prep_ct():
+        c_grads.wait()
+        x_grads.wait_recv()
+        ag[CT, y, x] = jnp.where(z == n_z - 1, tok[2], tok[4])
+
+    def prep_nf():
+        c_acts.wait()
+        x_acts.wait_recv()
+        tok[1] = jnp.where(z == 0, tok[1], tok[3])
+        inputs = tok[1].astype(F32)
+        ag[NF, y, x] = (inputs * inv_rms(inputs)).astype(BF16)
+
+    def make_pre():
+        c_win.wait()
+        exchange[2].wait_recv()
+        for c in range(2):
+            value, grad = gelu_and_slope(nt(rows(NB), win[c]))
+            hid[c] = value.astype(BF16)
+            slope[c] = grad
+
+    def make_dpre():
+        c_wout.wait()
+        exchange[3].wait_recv()
+        for c in range(2):
+            dpre[c] = (nt(rows(CT), wout[c]) * slope[c]).astype(BF16)
+
+    def make_bwd(h):
         for s in range(2):
             csl = cols(h, s)
             part[BWD, :, :, :, csl] = (
-                (nt(dpre[0], win[0, csl, :]) + nt(dpre[1], win[1, csl, :])).astype(BF16).reshape(4, 4, 16, Q)
+                (nn(dpre[0], win[0, :, csl]) + nn(dpre[1], win[1, :, csl])).astype(BF16).reshape(4, 4, 16, Q)
             )
         rs0(BWD, h)
-    gather(NF, 6)
-    for c in range(2):
-        hid_f = gelu(nn(rows(NF), win[c])).astype(BF16)
-        slope[c] = hid_f.astype(F32)
-    scatter(BWD, 1)
-    for h in range(2):
+
+    def make_hidden():
+        for c in range(2):
+            fwd_hid[c] = gelu(nt(rows(NF), win[c])).astype(BF16)
+
+    def make_fwd(h):
         for s in range(2):
             csl = cols(h, s)
             part[FWD, :, :, :, csl] = (
-                (nn(slope[0].astype(BF16), wout[0, :, csl]) + nn(slope[1].astype(BF16), wout[1, :, csl]))
-                .astype(BF16).reshape(4, 4, 16, Q)
+                (nn(fwd_hid[0], wout[0, :, csl]) + nn(fwd_hid[1], wout[1, :, csl])).astype(BF16).reshape(4, 4, 16, Q)
             )
         rs0(FWD, h)
+
+    def give_gin():
+        gin_s[...] = tn(dpre[1], rows(NB)).astype(BF16)
+        exchange[4] = send(gin_s, gin_r, ex_send.at[4], ex_recv.at[4], sibling)
+
+    def give_gout():
+        gout_s[...] = tn(hid[1], rows(CT)).astype(BF16)
+        exchange[5] = send(gout_s, gout_r, ex_send.at[5], ex_recv.at[5], sibling)
+
+    def keep_grads():
+        o_gin[0] = tn(dpre[0], rows(NB)).astype(BF16)
+        o_gout[0] = tn(hid[0], rows(CT)).astype(BF16)
+
+    def add_grads():
+        exchange[4].wait_recv()
+        o_gin[0] = (o_gin[0].astype(F32) + gin_r[...].astype(F32)).astype(BF16)
+        exchange[5].wait_recv()
+        o_gout[0] = (o_gout[0].astype(F32) + gout_r[...].astype(F32)).astype(BF16)
+
+    exchange = {}
+
+    def meet_sibling():
+        exchange[2] = send(w_in.at[0], win.at[1], ex_send.at[2], ex_recv.at[2], sibling)
+        exchange[3] = send(w_out.at[0], wout.at[1], ex_send.at[3], ex_recv.at[3], sibling)
+
+    def finish_bwd():
+        d_normed = jnp.concatenate([rs4(BWD, 0), rs4(BWD, 1)], axis=-1)
+        kept = tok[0].astype(F32)
+        scale = inv_rms(kept)
+        inner = jnp.mean(d_normed * kept, axis=-1, keepdims=True)
+        back = scale * d_normed - kept * (scale * scale * scale * inner)
+        o_grads[0] = (ag[CT, y, x].astype(F32) + back).astype(BF16)
+
+    def finish_fwd():
+        o_acts[0] = (tok[1].astype(F32) + jnp.concatenate([rs4(FWD, 0), rs4(FWD, 1)], axis=-1)).astype(BF16)
+
+    prep_nb()
+    gather(NB, 0)
+    meet_sibling()
+    prep_ct()
+    gather(CT, 0)
+    prep_nf()
+    gather(NF, 0)
+    gather(NB, 1)
+    gather(CT, 1)
+    gather(NF, 1)
+    gather(NB, 2)
+    gather(CT, 2)
+    gather(NF, 2)
+    gather(NB, 3)
+    gather(CT, 3)
+    gather(NF, 3)
+    gather(NB, 4)
+    gather(CT, 4)
+    gather(NF, 4)
+    gather(NB, 5)
+    gather(CT, 5)
+    gather(NF, 5)
+    gather(NB, 6)
+    make_pre()
+    gather(CT, 6)
+    make_dpre()
+    make_bwd(0)
+    make_bwd(1)
+    gather(NF, 6)
+    make_hidden()
+    make_fwd(0)
+    make_fwd(1)
+    scatter(BWD, 1)
+    scatter(FWD, 1)
+    give_gin()
     scatter(BWD, 2)
-    gin_s[...] = tn(rows(NB), dpre[1]).astype(BF16)
-    x_gin = send(gin_s, gin_r, ex_send.at[4], ex_recv.at[4], sibling)
+    give_gout()
+    scatter(FWD, 2)
     scatter(BWD, 3)
-    scatter(FWD, 1)
-    gout_s[...] = tn(hid[1], rows(CT)).astype(BF16)
-    x_gout = send(gout_s, gout_r, ex_send.at[5], ex_recv.at[5], sibling)
-    scatter(FWD, 2)
-    gin_o[...] = tn(rows(NB), dpre[0]).astype(BF16)
-    gout_o[...] = tn(hid[0], rows(CT)).astype(BF16)
     scatter(FWD, 3)
-    x_gin.wait_recv()
-    gin_o[...] = (gin_o[...].astype(F32) + gin_r[...].astype(F32)).astype(BF16)
-    out_gin = pltpu.make_async_copy(gin_o, o_gin.at[0], loc_sem.at[5])
-    out_gin.start()
-    x_gout.wait_recv()
-    gout_o[...] = (gout_o[...].astype(F32) + gout_r[...].astype(F32)).astype(BF16)
-    out_gout = pltpu.make_async_copy(gout_o, o_gout.at[0], loc_sem.at[6])
-    out_gout.start()
-
-    d_normed = jnp.concatenate([rs4(BWD, 0), rs4(BWD, 1)], axis=-1)
-    kept = tok[0].astype(F32)
-    scale = inv_rms(kept)
-    inner = jnp.mean(d_normed * kept, axis=-1, keepdims=True)
-    back = scale * d_normed - kept * (scale * scale * scale * inner)
-    o_grads[0] = (ag[CT, y, x].astype(F32) + back).astype(BF16)
-    o_acts[0] = (tok[1].astype(F32) + jnp.concatenate([rs4(FWD, 0), rs4(FWD, 1)], axis=-1)).astype(BF16)
-    out_gin.wait()
-    out_gout.wait()
+    keep_grads()
+    finish_bwd()
+    finish_fwd()
+    add_grads()
     for copy in sent:
         copy.wait_send()
 
 
+def store(*refs):
+    copies = [pltpu.make_async_copy(refs[i], refs[4 + i], refs[8].at[i]) for i in range(4)]
+    for copy in copies:
+        copy.start()
+    for copy in copies:
+        copy.wait()
+
+
 def shards(n_z, acts, grads, saved, w_in, w_out):
     _, T, D = acts.shape
-    U = w_in.shape[2]
+    w_in = jnp.swapaxes(w_in, 1, 2)
+    U = w_in.shape[1]
     H, Q = D // 2, D // 4
     vmem = pltpu.VMEM
     sem = pltpu.SemaphoreType.DMA
     anywhere = pl.BlockSpec(memory_space=pl.ANY)
     whole = pl.BlockSpec(memory_space=pltpu.VMEM)
     tokens = 16 * T
-    return pl.pallas_call(
+    results = pl.pallas_call(
         functools.partial(kernel, n_z),
         out_shape=(
-            jax.ShapeDtypeStruct(acts.shape, BF16),
-            jax.ShapeDtypeStruct(acts.shape, BF16),
-            jax.ShapeDtypeStruct(w_in.shape, BF16),
-            jax.ShapeDtypeStruct(w_out.shape, BF16),
+            vmem(acts.shape, BF16),
+            vmem(acts.shape, BF16),
+            vmem(w_in.shape, BF16),
+            vmem(w_out.shape, BF16),
         ),
         in_specs=[anywhere] * 5,
-        out_specs=(whole, whole, anywhere, anywhere),
+        out_specs=(whole,) * 4,
         scratch_shapes=[
             vmem((5, T, D), BF16),
             vmem((3, 4, 4, T, D), BF16),
-            vmem((2, D, U), BF16),
+            vmem((2, U, D), BF16),
             vmem((2, U, D), BF16),
             vmem((2, 4, 4, T, D), BF16),
             vmem((2, 2, 2, 4, T, Q), BF16),
@@ -367,14 +413,13 @@
             vmem((2, 2, 4, T, H), BF16),
             vmem((2, tokens, U), BF16),
             vmem((2, tokens, U), BF16),
+            vmem((2, tokens, U), BF16),
             vmem((2, tokens, U), F32),
-            vmem((D, U), BF16),
-            vmem((D, U), BF16),
             vmem((U, D), BF16),
             vmem((U, D), BF16),
-            vmem((D, U), BF16),
             vmem((U, D), BF16),
-            sem((7,)),
+            vmem((U, D), BF16),
+            sem((5,)),
             sem((3, 2, 20)),
             sem((3, 2, 20)),
             sem((2, 2, 12)),
@@ -386,6 +431,15 @@
             collective_id=0, has_side_effects=True, vmem_limit_bytes=56 * 1024 * 1024
         ),
     )(acts, grads, saved, w_in, w_out)
+    out_acts, out_grads, grad_in, grad_out = pl.pallas_call(
+        store,
+        out_shape=tuple(jax.ShapeDtypeStruct(r.shape, r.dtype) for r in results),
+        in_specs=[anywhere] * 4,
+        out_specs=(anywhere,) * 4,
+        scratch_shapes=[sem((4,))],
+        compiler_params=pltpu.CompilerParams(vmem_limit_bytes=1024 * 1024),
+    )(*results)
+    return out_acts, out_grads, jnp.swapaxes(grad_in, 1, 2), grad_out
 
 
 def solution(mesh):

time: 83.5 us -> 68.1 us (0.82)
  the two profiles are of different devices: /device:TPU:8 before, /device:TPU:16 now
where the time goes in v2:
time: 68.1 us; the launch traced here: 67.9 us
  Pallas kernels  67.3 us (99%)
    pallas_call x1, Pallas kernels, shards(): pl.pallas_call(functools.partial(kernel, n_z), out_shape=(vmem(acts.shape...  65.8 us
    pallas_call x1, Pallas kernels, shards(): pl.pallas_call(store, out_shape=tuple((jax.ShapeDtypeStruct(r.shape, r.dt...  1.5 us

profile of v2, /device:TPU:16, one launch (start us, length us, event | category | flops | bytes accessed | tf_op | source)
XLA Modules:
  0.0 67.9 jit_solution(10015196366374377210)
XLA Ops:
  0.6 65.8 %shard_map.84 = (bf16[1,16,3072]{2,1,0:T(8,128)(2,1)S(1)}, bf16[1,16,3072]{2,1,0:T(8,128)(2,1)S(1)}, bf16[1,192,3072]{2,1,0:T(8,128)(2,1)S(1)}, bf16[1,192,3072]{2,1,0:T(8,128)(2,1)S(1)}) custom-call(bf16[1,16,3072]{2,1,0:T(8,128)(2,1)} %acts.1, bf16[1,16,3072]{2,1,0:T(8,128)(2,1)} %grads.1, bf16[1,16,3072]{2,1,0:T(8,128)(2,1)} %saved.1, ...), custom_call_target="tpu_custom_call" | custom-call | tf_op jit(solution)/shard_map/pallas_call | solution.py:393
  66.4 1.5 %shard_map.85 = (bf16[1,16,3072]{2,1,0:T(8,128)(2,1)}, bf16[1,16,3072]{2,1,0:T(8,128)(2,1)}, bf16[1,192,3072]{2,1,0:T(8,128)(2,1)}, bf16[1,192,3072]{2,1,0:T(8,128)(2,1)}) custom-call(bf16[1,16,3072]{2,1,0:T(8,128)(2,1)S(1)} %get-tuple-element.12.refs_0_, bf16[1,16,3072]{2,1,0:T(8,128)(2,1)S(1)} %get-tuple-element.13.refs_1_, ...), custom_call_target="tpu_custom_call" | custom-call | tf_op jit(solution)/shard_map/pallas_call | solution.py:434

commit v3 on v2

--- a/solution.py
+++ b/solution.py
@@ -45,7 +45,7 @@
 
 def kernel(
     n_z, acts, grads, saved, w_in, w_out, o_acts, o_grads, o_gin, o_gout,
-    tok, ag, win, wout, part, r1, r2, r3, r4, q, hid, fwd_hid, dpre, slope, gin_s, gin_r, gout_s, gout_r,
+    tok, ag, win, wout, part, r1, r2, r4, q, hid, fwd_hid, dpre, slope, gin_s, gin_r, gout_s, gout_r,
     loc_sem, ag_send, ag_recv, rs_send, rs_recv, ex_send, ex_recv,
 ):
     sec, y, dp = lax.axis_index("section"), lax.axis_index("tensor"), lax.axis_index("dp")
@@ -65,7 +65,7 @@
         return ((xx // 2) * n_z + z, yy, 2 * lax.rem(xx, 2) + core)
 
     def plane(dz):
-        return (x_hi * n_z + lax.rem(z + dz + n_z, n_z), y, dp)
+        return (sec + dz, y, dp)
 
     sibling = (sec, y, dp + 1 - 2 * core)
 
@@ -90,14 +90,29 @@
     c_win = local(w_in.at[0], win.at[0], 3)
     c_wout = local(w_out.at[0], wout.at[0], 4)
 
-    partners = [chip(0, 1), chip(0, -1), chip(1, 0), chip(-1, 0), plane(1), plane(-1), sibling]
+    has_next, has_last = z < n_z - 1, z > 0
     barrier = pltpu.get_barrier_semaphore()
-    for dev in partners:
+
+    def greet(dev):
         pl.semaphore_signal(barrier, inc=1, device_id=dev, device_id_type=MESH)
-    pl.semaphore_wait(barrier, len(partners))
-
-    x_acts = send(acts.at[0], tok.at[3], ex_send.at[0], ex_recv.at[0], plane(1))
-    x_grads = send(grads.at[0], tok.at[4], ex_send.at[1], ex_recv.at[1], plane(-1))
+
+    pl.when(has_next)(lambda: greet(plane(1)))
+    pl.when(has_last)(lambda: greet(plane(-1)))
+    for dev in (chip(0, 1), chip(0, -1), chip(1, 0), chip(-1, 0), sibling):
+        greet(dev)
+    pl.semaphore_wait(barrier, 5 + jnp.where(has_next, 1, 0) + jnp.where(has_last, 1, 0))
+
+    def shifted(src, dst, n, dev):
+        return pltpu.make_async_remote_copy(
+            src_ref=src, dst_ref=dst, send_sem=ex_send.at[n], recv_sem=ex_recv.at[n], device_id=dev,
+            device_id_type=MESH,
+        )
+
+    x_acts = shifted(acts.at[0], tok.at[3], 0, plane(1))
+    x_grads = shifted(grads.at[0], tok.at[4], 1, plane(-1))
+    pl.when(has_next)(x_acts.start)
+    pl.when(has_last)(x_grads.start)
+
     def cols(h, part_no=None):
         if part_no is None:
             return pl.ds(h * H, H)
@@ -200,36 +215,19 @@
         own = row(p, h, 0, cols(h))
         q[r, h] = (own[...].astype(F32) + r2[r, h, 0].astype(F32) + r2[r, h, 1].astype(F32)).astype(BF16)
 
-        def place(d):
-            return at(0, d)[1] if h == 0 else at(d, 0)[0]
-
-        for m, d in ((0, 1), (1, -1)):
-            rs_send_msg(
-                r, h, 6 + m, q.at[r, h, place(2), :, pl.ds(m * Q, Q)], r3.at[r, h, m], first(h, d)
-            )
-        for m, d in ((0, 1), (1, -1)):
-            rs_send_msg(
-                r, h, 8 + m, q.at[r, h, place(d), :, pl.ds((1 - m) * Q, Q)],
-                r4.at[r, h, m, :, pl.ds((1 - m) * Q, Q)], first(h, d),
-            )
-
-    def rs3(r, h):
-        def place(d):
-            return at(0, d)[1] if h == 0 else at(d, 0)[0]
-
-        for m, d in ((0, 1), (1, -1)):
-            rmsgs[r, h, 6 + m].wait_recv()
-            near = q.at[r, h, place(d), :, pl.ds(m * Q, Q)]
-            near[...] = (near[...].astype(F32) + r3[r, h, m].astype(F32)).astype(BF16)
-            rs_send_msg(r, h, 10 + m, near, r4.at[r, h, m, :, pl.ds(m * Q, Q)], first(h, d))
+        for m, d in ((0, 2), (1, 1), (2, -1)):
+            place = at(0, d)[1] if h == 0 else at(d, 0)[0]
+            rs_send_msg(r, h, 6 + m, q.at[r, h, place], r4.at[r, h, m], first(h, d))
 
     def rs4(r, h):
-        for m in range(8, 12):
+        for m in range(6, 9):
             rmsgs[r, h, m].wait_recv()
-        place = x if h == 0 else y
-        return q[r, h, place].astype(F32) + r4[r, h, 0].astype(F32) + r4[r, h, 1].astype(F32)
-
-    rs_stages = (rs0, rs1, rs2, rs3)
+        total = q[r, h, x if h == 0 else y].astype(F32)
+        for m in range(3):
+            total += r4[r, h, m].astype(F32)
+        return total
+
+    rs_stages = (rs0, rs1, rs2)
 
     def scatter(r, stage):
         for h in range(2):
@@ -245,13 +243,13 @@
 
     def prep_ct():
         c_grads.wait()
-        x_grads.wait_recv()
-        ag[CT, y, x] = jnp.where(z == n_z - 1, tok[2], tok[4])
+        pl.when(has_next)(x_grads.wait_recv)
+        ag[CT, y, x] = jnp.where(has_next, tok[4], tok[2])
 
     def prep_nf():
         c_acts.wait()
-        x_acts.wait_recv()
-        tok[1] = jnp.where(z == 0, tok[1], tok[3])
+        pl.when(has_last)(x_acts.wait_recv)
+        tok[1] = jnp.where(has_last, tok[3], tok[1])
         inputs = tok[1].astype(F32)
         ag[NF, y, x] = (inputs * inv_rms(inputs)).astype(BF16)
 
@@ -327,28 +325,28 @@
     prep_nb()
     gather(NB, 0)
     meet_sibling()
+    gather(NB, 1)
     prep_ct()
     gather(CT, 0)
+    gather(NB, 2)
     prep_nf()
     gather(NF, 0)
-    gather(NB, 1)
     gather(CT, 1)
+    gather(NB, 3)
     gather(NF, 1)
-    gather(NB, 2)
+    gather(NB, 4)
     gather(CT, 2)
     gather(NF, 2)
-    gather(NB, 3)
     gather(CT, 3)
+    gather(NB, 5)
+    gather(CT, 4)
     gather(NF, 3)
-    gather(NB, 4)
-    gather(CT, 4)
+    gather(NB, 6)
+    gather(CT, 5)
     gather(NF, 4)
-    gather(NB, 5)
-    gather(CT, 5)
-    gather(NF, 5)
-    gather(NB, 6)
     make_pre()
     gather(CT, 6)
+    gather(NF, 5)
     make_dpre()
     make_bwd(0)
     make_bwd(1)
@@ -357,17 +355,17 @@
     make_fwd(0)
     make_fwd(1)
     scatter(BWD, 1)
+    give_gin()
     scatter(FWD, 1)
-    give_gin()
+    give_gout()
     scatter(BWD, 2)
-    give_gout()
     scatter(FWD, 2)
-    scatter(BWD, 3)
-    scatter(FWD, 3)
     keep_grads()
+    add_grads()
     finish_bwd()
     finish_fwd()
-    add_grads()
+    pl.when(has_next)(x_acts.wait_send)
+    pl.when(has_last)(x_grads.wait_send)
     for copy in sent:
         copy.wait_send()
 
@@ -408,8 +406,7 @@
             vmem((2, 4, 4, T, D), BF16),
             vmem((2, 2, 2, 4, T, Q), BF16),
             vmem((2, 2, 2, 4, T, H), BF16),
-            vmem((2, 2, 2, T, Q), BF16),
-            vmem((2, 2, 2, T, H), BF16),
+            vmem((2, 2, 3, T, H), BF16),
             vmem((2, 2, 4, T, H), BF16),
             vmem((2, tokens, U), BF16),
             vmem((2, tokens, U), BF16),
@@ -422,8 +419,8 @@
             sem((5,)),
             sem((3, 2, 20)),
             sem((3, 2, 20)),
-            sem((2, 2, 12)),
-            sem((2, 2, 12)),
+            sem((2, 2, 9)),
+            sem((2, 2, 9)),
             sem((6,)),
             sem((6,)),
         ],

time: 68.1 us -> 60 us (0.88)
  the two profiles are of different devices: /device:TPU:16 before, /device:TPU:96 now
where the time goes in v3:
time: 60 us; the launch traced here: 59.9 us
  Pallas kernels  59.2 us (99%)
  between operations  0.64 us (1%)
    pallas_call x1, Pallas kernels, shards(): pl.pallas_call(functools.partial(kernel, n_z), out_shape=(vmem(acts.shape...  57.7 us
    pallas_call x1, Pallas kernels, shards(): pl.pallas_call(store, out_shape=tuple((jax.ShapeDtypeStruct(r.shape, r.dt...  1.5 us

profile of v3, /device:TPU:96, one launch (start us, length us, event | category | flops | bytes accessed | tf_op | source)
XLA Modules:
  0.0 59.9 jit_solution(7509884607528703616)
XLA Ops:
  0.6 57.7 %shard_map.84 = (bf16[1,16,3072]{2,1,0:T(8,128)(2,1)S(1)}, bf16[1,16,3072]{2,1,0:T(8,128)(2,1)S(1)}, bf16[1,192,3072]{2,1,0:T(8,128)(2,1)S(1)}, bf16[1,192,3072]{2,1,0:T(8,128)(2,1)S(1)}) custom-call(bf16[1,16,3072]{2,1,0:T(8,128)(2,1)} %acts.1, bf16[1,16,3072]{2,1,0:T(8,128)(2,1)} %grads.1, bf16[1,16,3072]{2,1,0:T(8,128)(2,1)} %saved.1, ...), custom_call_target="tpu_custom_call" | custom-call | tf_op jit(solution)/shard_map/pallas_call | solution.py:391
  58.4 1.5 %shard_map.85 = (bf16[1,16,3072]{2,1,0:T(8,128)(2,1)}, bf16[1,16,3072]{2,1,0:T(8,128)(2,1)}, bf16[1,192,3072]{2,1,0:T(8,128)(2,1)}, bf16[1,192,3072]{2,1,0:T(8,128)(2,1)}) custom-call(bf16[1,16,3072]{2,1,0:T(8,128)(2,1)S(1)} %get-tuple-element.12.refs_0_, bf16[1,16,3072]{2,1,0:T(8,128)(2,1)S(1)} %get-tuple-element.13.refs_1_, ...), custom_call_target="tpu_custom_call" | custom-call | tf_op jit(solution)/shard_map/pallas_call | solution.py:431

commit v4 on v3

--- a/solution.py
+++ b/solution.py
@@ -79,6 +79,17 @@
         sent.append(copy)
         return copy
 
+    has_next, has_last = z < n_z - 1, z > 0
+    barrier = pltpu.get_barrier_semaphore()
+
+    def greet(dev):
+        pl.semaphore_signal(barrier, inc=1, device_id=dev, device_id_type=MESH)
+
+    pl.when(has_next)(lambda: greet(plane(1)))
+    pl.when(has_last)(lambda: greet(plane(-1)))
+    for dev in (chip(0, 1), chip(0, -1), chip(1, 0), chip(-1, 0), sibling):
+        greet(dev)
+
     def local(src, dst, i):
         copy = pltpu.make_async_copy(src, dst, loc_sem.at[i])
         copy.start()
@@ -90,16 +101,10 @@
     c_win = local(w_in.at[0], win.at[0], 3)
     c_wout = local(w_out.at[0], wout.at[0], 4)
 
-    has_next, has_last = z < n_z - 1, z > 0
-    barrier = pltpu.get_barrier_semaphore()
-
-    def greet(dev):
-        pl.semaphore_signal(barrier, inc=1, device_id=dev, device_id_type=MESH)
-
-    pl.when(has_next)(lambda: greet(plane(1)))
-    pl.when(has_last)(lambda: greet(plane(-1)))
-    for dev in (chip(0, 1), chip(0, -1), chip(1, 0), chip(-1, 0), sibling):
-        greet(dev)
+    c_saved.wait()
+    kept = tok[0].astype(F32)
+    ag[NB, y, x] = (kept * inv_rms(kept)).astype(BF16)
+
     pl.semaphore_wait(barrier, 5 + jnp.where(has_next, 1, 0) + jnp.where(has_last, 1, 0))
 
     def shifted(src, dst, n, dev):
@@ -175,11 +180,6 @@
         for m in range(12, 20):
             msgs[k, h, m].wait_recv()
 
-    ag_stages = (ag0, ag1, ag2, ag3, ag4, ag5, ag6)
-
-    def gather(k, stage):
-        for h in range(2):
-            ag_stages[stage](k, h)
 
     def row(ref, h, d, csl):
         if h == 0:
@@ -227,19 +227,9 @@
             total += r4[r, h, m].astype(F32)
         return total
 
-    rs_stages = (rs0, rs1, rs2)
-
-    def scatter(r, stage):
-        for h in range(2):
-            rs_stages[stage](r, h)
 
     def rows(k):
         return ag[k].reshape(tokens, D)
-
-    def prep_nb():
-        c_saved.wait()
-        kept = tok[0].astype(F32)
-        ag[NB, y, x] = (kept * inv_rms(kept)).astype(BF16)
 
     def prep_ct():
         c_grads.wait()
@@ -322,45 +312,69 @@
     def finish_fwd():
         o_acts[0] = (tok[1].astype(F32) + jnp.concatenate([rs4(FWD, 0), rs4(FWD, 1)], axis=-1)).astype(BF16)
 
-    prep_nb()
-    gather(NB, 0)
+    ag0(NB, 0)
+    ag0(NB, 1)
     meet_sibling()
-    gather(NB, 1)
+    ag1(NB, 0)
+    ag1(NB, 1)
     prep_ct()
-    gather(CT, 0)
-    gather(NB, 2)
+    ag0(CT, 0)
+    ag0(CT, 1)
+    ag2(NB, 0)
+    ag2(NB, 1)
     prep_nf()
-    gather(NF, 0)
-    gather(CT, 1)
-    gather(NB, 3)
-    gather(NF, 1)
-    gather(NB, 4)
-    gather(CT, 2)
-    gather(NF, 2)
-    gather(CT, 3)
-    gather(NB, 5)
-    gather(CT, 4)
-    gather(NF, 3)
-    gather(NB, 6)
-    gather(CT, 5)
-    gather(NF, 4)
+    ag0(NF, 0)
+    ag0(NF, 1)
+    ag1(CT, 0)
+    ag1(CT, 1)
+    ag3(NB, 0)
+    ag3(NB, 1)
+    ag1(NF, 0)
+    ag1(NF, 1)
+    ag4(NB, 0)
+    ag4(NB, 1)
+    ag2(CT, 0)
+    ag2(CT, 1)
+    ag2(NF, 0)
+    ag2(NF, 1)
+    ag3(CT, 0)
+    ag3(CT, 1)
+    ag5(NB, 0)
+    ag5(NB, 1)
+    ag4(CT, 0)
+    ag4(CT, 1)
+    ag3(NF, 0)
+    ag3(NF, 1)
+    ag6(NB, 0)
+    ag6(NB, 1)
+    ag5(CT, 0)
+    ag5(CT, 1)
+    ag4(NF, 0)
+    ag4(NF, 1)
     make_pre()
-    gather(CT, 6)
-    gather(NF, 5)
+    ag6(CT, 0)
+    ag6(CT, 1)
+    ag5(NF, 0)
+    ag5(NF, 1)
     make_dpre()
     make_bwd(0)
     make_bwd(1)
-    gather(NF, 6)
+    give_gin()
+    ag6(NF, 0)
+    ag6(NF, 1)
     make_hidden()
     make_fwd(0)
     make_fwd(1)
-    scatter(BWD, 1)
-    give_gin()
-    scatter(FWD, 1)
+    rs1(BWD, 0)
+    rs1(BWD, 1)
     give_gout()
-    scatter(BWD, 2)
-    scatter(FWD, 2)
+    rs1(FWD, 0)
+    rs1(FWD, 1)
     keep_grads()
+    rs2(BWD, 0)
+    rs2(BWD, 1)
+    rs2(FWD, 0)
+    rs2(FWD, 1)
     add_grads()
     finish_bwd()
     finish_fwd()
@@ -371,7 +385,12 @@
 
 
 def store(*refs):
-    copies = [pltpu.make_async_copy(refs[i], refs[4 + i], refs[8].at[i]) for i in range(4)]
+    copies = []
+    for n, piece in enumerate((refs[0].shape[1], refs[1].shape[1], 48, 48)):
+        for at in range(0, refs[n].shape[1], piece):
+            rows = pl.ds(at, piece)
+            copies.append((refs[n].at[:, rows], refs[4 + n].at[:, rows]))
+    copies = [pltpu.make_async_copy(src, dst, refs[8].at[n]) for n, (src, dst) in enumerate(copies)]
     for copy in copies:
         copy.start()
     for copy in copies:
@@ -433,7 +452,7 @@
         out_shape=tuple(jax.ShapeDtypeStruct(r.shape, r.dtype) for r in results),
         in_specs=[anywhere] * 4,
         out_specs=(anywhere,) * 4,
-        scratch_shapes=[sem((4,))],
+        scratch_shapes=[sem((2 + 2 * (U // 48),))],
         compiler_params=pltpu.CompilerParams(vmem_limit_bytes=1024 * 1024),
     )(*results)
     return out_acts, out_grads, jnp.swapaxes(grad_in, 1, 2), grad_out

time: 60 us -> 59.9 us (level)
  no operation moved by 1% of the time
where the time goes in v4:
time: 59.9 us; the launch traced here: 59.8 us
  Pallas kernels  59.1 us (99%)
  between operations  0.64 us (1%)
    pallas_call x1, Pallas kernels, shards(): pl.pallas_call(functools.partial(kernel, n_z), out_shape=(vmem(acts.shape...  57.6 us
    pallas_call x1, Pallas kernels, shards(): pl.pallas_call(store, out_shape=tuple((jax.ShapeDtypeStruct(r.shape, r.dt...  1.55 us

profile of v4, /device:TPU:96, one launch (start us, length us, event | category | flops | bytes accessed | tf_op | source)
XLA Modules:
  0.0 59.8 jit_solution(280111267994604438)
XLA Ops:
  0.6 57.6 %shard_map.84 = (bf16[1,16,3072]{2,1,0:T(8,128)(2,1)S(1)}, bf16[1,16,3072]{2,1,0:T(8,128)(2,1)S(1)}, bf16[1,192,3072]{2,1,0:T(8,128)(2,1)S(1)}, bf16[1,192,3072]{2,1,0:T(8,128)(2,1)S(1)}) custom-call(bf16[1,16,3072]{2,1,0:T(8,128)(2,1)} %acts.1, bf16[1,16,3072]{2,1,0:T(8,128)(2,1)} %grads.1, bf16[1,16,3072]{2,1,0:T(8,128)(2,1)} %saved.1, ...), custom_call_target="tpu_custom_call" | custom-call | tf_op jit(solution)/shard_map/pallas_call | solution.py:410
  58.2 1.5 %shard_map.85 = (bf16[1,16,3072]{2,1,0:T(8,128)(2,1)}, bf16[1,16,3072]{2,1,0:T(8,128)(2,1)}, bf16[1,192,3072]{2,1,0:T(8,128)(2,1)}, bf16[1,192,3072]{2,1,0:T(8,128)(2,1)}) custom-call(bf16[1,16,3072]{2,1,0:T(8,128)(2,1)S(1)} %get-tuple-element.12.refs_0_, bf16[1,16,3072]{2,1,0:T(8,128)(2,1)S(1)} %get-tuple-element.13.refs_1_, ...), custom_call_target="tpu_custom_call" | custom-call | tf_op jit(solution)/shard_map/pallas_call | solution.py:450
